TPU v7x, 32 devices: a whole 2x2x4 slice. The times are simulated.
32 devices in a mesh: segment: 4 (over y, core), row: 2 (over x), dp: 4 (over z).
Axes of the slice: x: 2, y: 2, z: 4, core: 2. Of those that a mesh axis runs over, the one named last changes fastest.
Arguments:
- fresh: float32 [2, 4, 16, 16, 256], P(None, 'dp', 'row'), may hold values from -6 to 6
- target: float32 [1, 4, 16, 16, 256], P(None, 'dp', 'row'), may hold values from -6 to 6
- carried: float32 [4, 4, 16, 16, 256], P('segment', 'dp', 'row'), may hold values from -6 to 6
- returning: float32 [4, 2, 4, 16, 16, 256], P('segment', None, 'dp', 'row'), may hold values from -6 to 6
- weights: float32 [4, 2, 2, 1152, 128], P('segment'), may hold values from -0.09375 to 0.09375
- section_blocks: int32 [4], P('segment'), may hold values from 1 to 2, as said below
Outputs:
- grad_weights: float32 [4, 2, 2, 1152, 128], P('segment', None, None, ('row', 'dp'))
- leaving: float32 [4, 4, 16, 16, 256], P('segment', 'dp', 'row')
- sent_back: float32 [4, 2, 4, 16, 16, 256], P('segment', None, 'dp', 'row')
Inputs may be any that keep to these rules, and one draw needn't show every extreme that they name: `section_blocks`: each section holds one or two blocks; some section holds two and some one.
All inputs are finite; a program needn't handle non-finite values.
Results may differ from a plain program's by a relative error of at most 0.00012.
Values sent between devices are 32-bit elements; how exact they have to be, the bound alone decides.
A program may use at most 64 MiB of HBM per device.

v0:
```python
import math

import jax
import jax.numpy as jnp
from jax import lax
from jax.sharding import PartitionSpec as P

HIGHEST = lax.Precision.HIGHEST


def with_halo(block, sides, width):
    for axis, dim in sides:
        count = lax.axis_size(axis)
        forward = [(i, i + 1) for i in range(count - 1)]
        backward = [(target, source) for source, target in forward]
        low = lax.ppermute(
            lax.slice_in_dim(block, block.shape[dim] - width, None, axis=dim), axis, forward
        )
        high = lax.ppermute(lax.slice_in_dim(block, 0, width, axis=dim), axis, backward)
        block = jnp.concatenate([low, block, high], axis=dim)
    return block


def from_behind(value, axis, by):
    peers = lax.axis_size(axis)
    pairs = [(i, i + by) for i in range(peers) if 0 <= i + by < peers]
    return lax.ppermute(value, axis, pairs)


def matmul(left, right):
    return jnp.dot(left, right, precision=HIGHEST, preferred_element_type=jnp.float32)


def silu_slope(field):
    logistic = jax.nn.sigmoid(field)
    return logistic * (1.0 + field * (1.0 - logistic))


def neighbours(padded):
    rows_here = padded.shape[1] - 2
    cols_here = padded.shape[2]
    depth = padded.shape[3]
    widened = jnp.pad(padded, ((0, 0), (0, 0), (1, 1), (0, 0)))
    patches = [
        widened[:, row_tap : row_tap + rows_here, col_tap : col_tap + cols_here, :]
        for row_tap in range(3)
        for col_tap in range(3)
    ]
    return jnp.concatenate(patches, axis=3).reshape(-1, 9 * depth)


def flipped(kernel):
    chans = kernel.shape[1]
    return (
        kernel.reshape(3, 3, chans, chans)[::-1, ::-1]
        .transpose(0, 1, 3, 2)
        .reshape(9 * chans, chans)
    )


def joined_rim(field):
    return with_halo(field, (("row", 1),), 1)


def split_half(field):
    chans = field.shape[-1] // 2
    return (field[..., :chans], field[..., chans:])


def join_half(upper_half, lower_half):
    return jnp.concatenate([upper_half, lower_half], axis=-1)


def advance(resid, padded_source, kernel):
    return resid + matmul(neighbours(padded_source), kernel).reshape(resid.shape)


def pullback(source, cotangent, kernel, flip_kernel, padded_source, padded_cotangent):
    patches = neighbours(padded_source)
    rebuilt = matmul(patches, kernel).reshape(source.shape)
    kernel_grad = lax.dot_general(
        patches,
        cotangent.reshape(-1, cotangent.shape[-1]),
        (((0,), (0,)), ((), ())),
        precision=HIGHEST,
        preferred_element_type=jnp.float32,
    )
    field_grad = matmul(neighbours(padded_cotangent), flip_kernel).reshape(
        source.shape
    ) * silu_slope(source)
    return (rebuilt, field_grad, kernel_grad)


def tick_joined(source, outputs, grads, kernels, flips, doubled):
    fwd_upper, fwd_lower = split_half(source)
    back_upper, back_lower = split_half(outputs)
    grad_upper, grad_lower = split_half(grads)
    chans = fwd_upper.shape[-1]
    block_grads = [[None, None], [None, None]]
    saved_forward = source
    for step_id in range(4):
        fwd_block = step_id // 2
        back_block = 1 - step_id // 2
        is_even = step_id % 2 == 0
        if is_even:
            fwd_source, back_source, back_cotangent = (fwd_lower, back_upper, grad_lower)
        else:
            fwd_source, back_source, back_cotangent = (fwd_upper, back_lower, grad_upper)
        padded = joined_rim(
            jnp.concatenate(
                [jax.nn.silu(fwd_source), jax.nn.silu(back_source), back_cotangent], axis=-1
            )
        )
        padded_forward = padded[..., :chans]
        padded_source = padded[..., chans : 2 * chans]
        padded_cotangent = padded[..., 2 * chans :]
        if is_even:
            fwd_upper = advance(fwd_upper, padded_forward, kernels[fwd_block, 0])
            rebuilt, added_grad, kernel_grad = pullback(
                back_source,
                back_cotangent,
                kernels[back_block, 1],
                flips[back_block][1],
                padded_source,
                padded_cotangent,
            )
            back_lower = back_lower - rebuilt
            grad_upper = grad_upper + added_grad
            block_grads[back_block][1] = kernel_grad
        else:
            fwd_lower = advance(fwd_lower, padded_forward, kernels[fwd_block, 1])
            rebuilt, added_grad, kernel_grad = pullback(
                back_source,
                back_cotangent,
                kernels[back_block, 0],
                flips[back_block][0],
                padded_source,
                padded_cotangent,
            )
            back_upper = back_upper - rebuilt
            grad_lower = grad_lower + added_grad
            block_grads[back_block][0] = kernel_grad
        if step_id == 1:
            saved_forward = join_half(fwd_upper, fwd_lower)
            kept_outputs = jnp.where(doubled, join_half(back_upper, back_lower), outputs)
            kept_grads = jnp.where(doubled, join_half(grad_upper, grad_lower), grads)
            back_upper, back_lower = split_half(kept_outputs)
            grad_upper, grad_lower = split_half(kept_grads)
    produced = jnp.where(doubled, join_half(fwd_upper, fwd_lower), saved_forward)
    factor = doubled.astype(jnp.float32)
    tick_grads = jnp.stack([jnp.stack(block_grads[0]), jnp.stack(block_grads[1]) * factor])
    return (
        produced,
        join_half(back_upper, back_lower),
        join_half(grad_upper, grad_lower),
        tick_grads,
    )


def per_device(fresh, target, carried, returning, weights, section_blocks):
    segment_id = lax.axis_index("segment")
    segment_count = lax.axis_size("segment")
    is_first = segment_id == 0
    is_final = segment_id == segment_count - 1
    doubled = section_blocks[0] == 2
    kernels = weights[0]
    flips = [[flipped(kernels[block_id, half_id]) for half_id in range(2)] for block_id in range(2)]
    cells = (
        fresh.shape[0]
        * fresh.shape[1]
        * lax.axis_size("dp")
        * fresh.shape[2]
        * lax.axis_size("row")
        * fresh.shape[3]
    )
    tick_count = fresh.shape[0]
    incoming = carried[0]
    returned = returning[0]
    running = None
    produced = incoming
    rebuilt_in = incoming
    grad_in = incoming
    for window_tick in range(tick_count):
        source = jnp.where(is_first, fresh[window_tick], incoming)
        produced, rebuilt_in, grad_in, tick_grads = tick_joined(
            source, returned[0], returned[1], kernels, flips, doubled
        )
        running = tick_grads if running is None else running + tick_grads
        if window_tick < tick_count - 1:
            incoming = from_behind(produced, "segment", 1)
            shifted = from_behind(jnp.stack([rebuilt_in, grad_in]), "segment", -1)
            own_pair = jnp.stack([produced, produced - target[window_tick]])
            returned = jnp.where(is_final, own_pair, shifted)
    totals = lax.psum_scatter(running, ("row", "dp"), scatter_dimension=2, tiled=True)
    grad_weights = (totals / math.sqrt(cells))[None]
    return (grad_weights, produced[None], jnp.stack([rebuilt_in, grad_in])[None])


def solution(mesh):
    return jax.shard_map(
        per_device,
        mesh=mesh,
        in_specs=(
            P(None, "dp", "row", None, None),
            P(None, "dp", "row", None, None),
            P("segment", "dp", "row", None, None),
            P("segment", None, "dp", "row", None, None),
            P("segment", None, None, None, None),
            P("segment"),
        ),
        out_specs=(
            P("segment", None, None, ("row", "dp"), None),
            P("segment", "dp", "row", None, None),
            P("segment", None, "dp", "row", None, None),
        ),
        check_vma=False,
    )
```

profile of v0, /device:TPU:1, one launch (start us, length us, event | category | flops | bytes accessed | tf_op | source)
XLA Modules:
  0.0 198.1 jit_solution(16437651244275762954)
XLA Ops:
  7.2 1.6 select_bitcast_fusion
  8.9 0.9 divide_multiply_fusion.7
  9.7 1.0 slice_bitcast_fusion.3
  12.1 4.5 %collective-permute-start = (f32[1,1,16,384]{3,2,1,0:T(8,128)}, f32[1,1,16,384]{3,2,1,0:T(8,128)}, u32[]{:S(2)}, u32[]{:S(2)}) collective-permute-start(f32[1,1,16,384]{3,2,1,0:T(8,128)} %get-tuple-element.108), channel_id=1, source_target_pairs={{0,4},{1,5},{2,6},{3,7},{8,12},{9,13},{10,14},{11,15},{16,20},{17,... | collective-permute-start | bytes 73736 | tf_op jit(solution)/shard_map/ppermute | solution.py:16
  16.6 1.3 collective-permute-start.1
  18.0 1.8 fusion.126
  20.8 1.1 copy.10
  22.1 1.1 copy.9
  23.2 1.1 pad_maximum_fusion.1
  24.4 0.9 constant_dynamic-update-slice_fusion.7
  25.3 0.9 constant_dynamic-update-slice_fusion.4
  26.5 0.7 constant_dynamic-update-slice_fusion.1
  27.3 1.5 divide_multiply_fusion.6
  28.8 0.7 fusion.94
  29.6 0.7 fusion.13
  30.3 4.6 %collective-permute-start.2 = (f32[1,1,16,384]{3,2,1,0:T(8,128)S(1)}, f32[1,1,16,384]{3,2,1,0:T(8,128)S(1)}, u32[]{:S(2)}, u32[]{:S(2)}) collective-permute-start(f32[1,1,16,384]{3,2,1,0:T(8,128)S(1)} %get-tuple-element.106), channel_id=1, source_target_pairs={{0,4},{1,5},{2,6},{3,7},{8,12},{9,13},{10,14},{11,15},{16,20},{17,... | collective-permute-start | bytes 73736 | tf_op jit(solution)/shard_map/ppermute | solution.py:16
  34.9 1.3 collective-permute-start.3
  36.2 1.1 convolution_bitcast_fusion.4
  37.3 2.2 %collective-permute-done.3 = f32[1,1,16,384]{3,2,1,0:T(8,128)S(1)} collective-permute-done((f32[1,1,16,384]{3,2,1,0:T(8,128)S(1)}, f32[1,1,16,384]{3,2,1,0:T(8,128)S(1)}, u32[]{:S(2)}, u32[]{:S(2)}) %collective-permute-start.3) | collective-permute-done | bytes 24608 | tf_op jit(solution)/shard_map/ppermute | solution.py:19
  40.6 1.1 convolution_bitcast_fusion.5
  41.7 1.5 divide_multiply_fusion.5
  44.1 1.8 collective-permute-start.4
  46.0 1.5 collective-permute-start.5
  47.5 3.0 %collective-permute-done.5 = f32[1,1,16,384]{3,2,1,0:T(8,128)S(1)} collective-permute-done((f32[1,1,16,384]{3,2,1,0:T(8,128)S(1)}, f32[1,1,16,384]{3,2,1,0:T(8,128)S(1)}, u32[]{:S(2)}, u32[]{:S(2)}) %collective-permute-start.5) | collective-permute-done | bytes 24608 | tf_op jit(solution)/shard_map/ppermute | solution.py:19
  51.0 0.7 divide_multiply_fusion.4
  51.7 0.7 fusion.92
  52.5 0.7 fusion.9
  53.2 1.6 collective-permute-start.6
  54.8 1.3 collective-permute-start.7
  56.1 1.1 convolution_bitcast_fusion.6
  57.2 2.2 %collective-permute-done.7 = f32[1,1,16,384]{3,2,1,0:T(8,128)S(1)} collective-permute-done((f32[1,1,16,384]{3,2,1,0:T(8,128)S(1)}, f32[1,1,16,384]{3,2,1,0:T(8,128)S(1)}, u32[]{:S(2)}, u32[]{:S(2)}) %collective-permute-start.7) | collective-permute-done | bytes 24608 | tf_op jit(solution)/shard_map/ppermute | solution.py:19
  60.5 1.1 convolution_bitcast_fusion.7
  62.4 7.8 %collective-permute-start.8 = (f32[1,8,16,256]{3,2,1,0:T(8,128)S(1)}, f32[1,8,16,256]{3,2,1,0:T(8,128)S(1)}, u32[]{:S(2)}, u32[]{:S(2)}) collective-permute-start(f32[1,8,16,256]{3,2,1,0:T(8,128)S(1)} %maximum_select_fusion.3), channel_id=1, source_target_pairs={{0,8},{8,16},{16,24},{1,9},{9,17},{17,25},{2,10},{10,18},{18,26},{... | collective-permute-start | bytes 393224 | tf_op jit(solution)/shard_map/ppermute | solution.py:27
  71.0 1.9 collective-permute-start.9
  73.0 5.6 %collective-permute-done.9 = f32[2,1,8,16,256]{4,3,2,1,0:T(8,128)S(1)} collective-permute-done((f32[2,1,8,16,256]{4,3,2,1,0:T(8,128)S(1)}, f32[2,1,8,16,256]{4,3,2,1,0:T(8,128)S(1)}, u32[]{:S(2)}, u32[]{:S(2)}) %collective-permute-start.9) | collective-permute-done | bytes 262176 | tf_op jit(solution)/shard_map/ppermute | solution.py:27
  78.8 1.3 collective-permute-start.10
  80.1 1.3 collective-permute-start.11
  81.5 3.2 %collective-permute-done.11 = f32[1,1,16,384]{3,2,1,0:T(8,128)S(1)} collective-permute-done((f32[1,1,16,384]{3,2,1,0:T(8,128)S(1)}, f32[1,1,16,384]{3,2,1,0:T(8,128)S(1)}, u32[]{:S(2)}, u32[]{:S(2)}) %collective-permute-start.11) | collective-permute-done | bytes 24608 | tf_op jit(solution)/shard_map/ppermute | solution.py:19
  86.5 0.7 fusion.90
  87.2 0.7 slice_add_fusion.1
  87.9 1.6 collective-permute-start.12
  89.6 1.5 collective-permute-start.13
  91.1 1.1 convolution_bitcast_fusion
  92.2 1.9 collective-permute-done.13
  95.3 1.1 convolution_bitcast_fusion.1
  96.4 0.7 divide_multiply_fusion.1
  98.0 2.1 %collective-permute-start.14 = (f32[1,1,16,384]{3,2,1,0:T(8,128)S(1)}, f32[1,1,16,384]{3,2,1,0:T(8,128)S(1)}, u32[]{:S(2)}, u32[]{:S(2)}) collective-permute-start(f32[1,1,16,384]{3,2,1,0:T(8,128)S(1)} %get-tuple-element.96), channel_id=1, source_target_pairs={{0,4},{1,5},{2,6},{3,7},{8,12},{9,13},{10,14},{11,15},{16,20},{17,... | collective-permute-start | bytes 73736 | tf_op jit(solution)/shard_map/ppermute | solution.py:16
  100.1 1.3 collective-permute-start.15
  101.5 3.2 %collective-permute-done.15 = f32[1,1,16,384]{3,2,1,0:T(8,128)S(1)} collective-permute-done((f32[1,1,16,384]{3,2,1,0:T(8,128)S(1)}, f32[1,1,16,384]{3,2,1,0:T(8,128)S(1)}, u32[]{:S(2)}, u32[]{:S(2)}) %collective-permute-start.15) | collective-permute-done | bytes 24608 | tf_op jit(solution)/shard_map/ppermute | solution.py:19
  105.1 0.7 divide_multiply_fusion
  105.8 0.7 fusion.86
  107.3 1.6 collective-permute-start.16
  109.0 1.6 collective-permute-start.17
  110.5 1.1 convolution_bitcast_fusion.2
  111.6 1.9 collective-permute-done.17
  114.0 0.8 copy-done.24
  115.0 0.8 copy-done.26
  115.9 1.1 convolution_bitcast_fusion.3
  117.0 1.6 maximum_add_fusion
  120.0 1.8 fusion.1
  121.9 1.7 fusion.27
  125.1 0.7 maximum_bitcast_fusion.2
  125.8 63.8 %reduce-scatter.2.cloned.1.call-done = f32[2,2,144,128]{3,2,1,0:T(8,128)} async-done(((f32[2,2,1152,128]{3,2,1,0:T(8,128)}), f32[2,2,144,128]{3,2,1,0:T(8,128)}) %reduce-scatter.2.cloned.1.call-update) | async-done | bytes 294928 | tf_op jit(solution)/shard_map/reduce_scatter | solution.py:194
  189.6 1.7 multiply_bitcast_fusion
  (322 shorter events, 14.8 us)
Async XLA Ops:
  7.2 182.4 %reduce-scatter.2.cloned.1.call-start = ((), (), s32[]{:S(2)}) async-start(), calls=%async_computation.1 | async-start | bytes 2654208 | tf_op jit(solution)/shard_map/reduce_scatter | solution.py:194
  9.7 8.2 %copy-start.5 = (f32[1,8,16,128]{3,2,1,0:T(8,128)}, f32[1,8,16,128]{3,2,1,0:T(8,128)S(1)}, u32[]{:S(2)}) copy-start(f32[1,8,16,128]{3,2,1,0:T(8,128)S(1)} %divide_multiply_fusion.7) | copy-start | bytes 196612
  10.8 0.7 copy-start.13
  10.8 7.2 %copy-start.17 = (f32[1,8,16,256]{3,2,1,0:T(8,128)}, f32[1,8,16,256]{3,2,1,0:T(8,128)S(1)}, u32[]{:S(2)}) copy-start(f32[1,8,16,256]{3,2,1,0:T(8,128)S(1)} %get-tuple-element.19) | copy-start | bytes 393220
  11.4 6.5 %copy-start.7 = (f32[1,8,16,128]{3,2,1,0:T(8,128)}, f32[1,8,16,128]{3,2,1,0:T(8,128)S(1)}, u32[]{:S(2)}) copy-start(f32[1,8,16,128]{3,2,1,0:T(8,128)S(1)} %fusion.95) | copy-start | bytes 196612
  11.4 6.5 %copy-start.9 = (f32[1,8,16,128]{3,2,1,0:T(8,128)}, f32[1,8,16,128]{3,2,1,0:T(8,128)S(1)}, u32[]{:S(2)}) copy-start(f32[1,8,16,128]{3,2,1,0:T(8,128)S(1)} %slice.1309) | copy-start | bytes 196612
  12.1 11.1 %collective-permute-start = (f32[1,1,16,384]{3,2,1,0:T(8,128)}, f32[1,1,16,384]{3,2,1,0:T(8,128)}, u32[]{:S(2)}, u32[]{:S(2)}) collective-permute-start(f32[1,1,16,384]{3,2,1,0:T(8,128)} %get-tuple-element.108), channel_id=1, source_target_pairs={{0,4},{1,5},{2,6},{3,7},{8,12},{9,13},{10,14},{11,15},{16,20},{17,... | collective-permute-start | bytes 73736 | tf_op jit(solution)/shard_map/ppermute | solution.py:16
  16.6 6.6 %collective-permute-start.1 = (f32[1,1,16,384]{3,2,1,0:T(8,128)}, f32[1,1,16,384]{3,2,1,0:T(8,128)}, u32[]{:S(2)}, u32[]{:S(2)}) collective-permute-start(f32[1,1,16,384]{3,2,1,0:T(8,128)} %get-tuple-element.109), channel_id=1, source_target_pairs={{4,0},{5,1},{6,2},{7,3},{12,8},{13,9},{14,10},{15,11},{20,16},{21,... | collective-permute-start | bytes 73736 | tf_op jit(solution)/shard_map/ppermute | solution.py:19
  23.1 3.2 %copy-start.14 = (f32[1,8,16,256]{3,2,1,0:T(8,128)S(1)}, f32[1,8,16,256]{3,2,1,0:T(8,128)}, u32[]{:S(2)}) copy-start(f32[1,8,16,256]{3,2,1,0:T(8,128)} %copy-done.13) | copy-start | bytes 393220
  23.1 3.2 %copy-start.18 = (f32[1,8,16,256]{3,2,1,0:T(8,128)S(1)}, f32[1,8,16,256]{3,2,1,0:T(8,128)}, u32[]{:S(2)}) copy-start(f32[1,8,16,256]{3,2,1,0:T(8,128)} %copy-done.17) | copy-start | bytes 393220
  23.1 3.3 %copy-start.6 = (f32[1,8,16,128]{3,2,1,0:T(8,128)S(1)}, f32[1,8,16,128]{3,2,1,0:T(8,128)}, u32[]{:S(2)}) copy-start(f32[1,8,16,128]{3,2,1,0:T(8,128)} %copy-done.5) | copy-start | bytes 196612
  23.2 3.3 %copy-start.8 = (f32[1,8,16,128]{3,2,1,0:T(8,128)S(1)}, f32[1,8,16,128]{3,2,1,0:T(8,128)}, u32[]{:S(2)}) copy-start(f32[1,8,16,128]{3,2,1,0:T(8,128)} %copy-done.7) | copy-start | bytes 196612
  23.2 3.3 %copy-start.10 = (f32[1,8,16,128]{3,2,1,0:T(8,128)S(1)}, f32[1,8,16,128]{3,2,1,0:T(8,128)}, u32[]{:S(2)}) copy-start(f32[1,8,16,128]{3,2,1,0:T(8,128)} %copy-done.9) | copy-start | bytes 196612
  23.2 4.1 %copy-start = (f32[1,2,2,1152,128]{4,3,2,1,0:T(8,128)S(1)}, f32[1,2,2,1152,128]{4,3,2,1,0:T(8,128)}, u32[]{:S(2)}) copy-start(f32[1,2,2,1152,128]{4,3,2,1,0:T(8,128)} %param.10) | copy-start | bytes 7077892
  26.3 3.3 %copy-start.2 = (f32[3,3,128,128]{3,2,1,0:T(8,128)S(1)}, f32[3,3,128,128]{3,2,1,0:T(8,128)}, u32[]{:S(2)}) copy-start(f32[3,3,128,128]{3,2,1,0:T(8,128)} %copy.9) | copy-start | bytes 1769476
  30.3 7.0 %collective-permute-start.2 = (f32[1,1,16,384]{3,2,1,0:T(8,128)S(1)}, f32[1,1,16,384]{3,2,1,0:T(8,128)S(1)}, u32[]{:S(2)}, u32[]{:S(2)}) collective-permute-start(f32[1,1,16,384]{3,2,1,0:T(8,128)S(1)} %get-tuple-element.106), channel_id=1, source_target_pairs={{0,4},{1,5},{2,6},{3,7},{8,12},{9,13},{10,14},{11,15},{16,20},{17,... | collective-permute-start | bytes 73736 | tf_op jit(solution)/shard_map/ppermute | solution.py:16
  34.9 4.6 %collective-permute-start.3 = (f32[1,1,16,384]{3,2,1,0:T(8,128)S(1)}, f32[1,1,16,384]{3,2,1,0:T(8,128)S(1)}, u32[]{:S(2)}, u32[]{:S(2)}) collective-permute-start(f32[1,1,16,384]{3,2,1,0:T(8,128)S(1)} %get-tuple-element.107), channel_id=1, source_target_pairs={{4,0},{5,1},{6,2},{7,3},{12,8},{13,9},{14,10},{15,11},{20,16},{21,... | collective-permute-start | bytes 73736 | tf_op jit(solution)/shard_map/ppermute | solution.py:19
  39.9 3.4 %copy-start.1 = (f32[3,3,128,128]{3,2,1,0:T(8,128)S(1)}, f32[3,3,128,128]{3,2,1,0:T(8,128)}, u32[]{:S(2)}) copy-start(f32[3,3,128,128]{3,2,1,0:T(8,128)} %copy.10) | copy-start | bytes 1769476
  40.6 3.4 %copy-start.19 = (f32[1,2,1,8,16,256]{5,4,3,2,1,0:T(8,128)S(1)}, f32[1,2,1,8,16,256]{5,4,3,2,1,0:T(8,128)}, u32[]{:S(2)}) copy-start(f32[1,2,1,8,16,256]{5,4,3,2,1,0:T(8,128)} %param.9) | copy-start | bytes 786436
  44.1 3.4 %collective-permute-start.4 = (f32[1,1,16,384]{3,2,1,0:T(8,128)S(1)}, f32[1,1,16,384]{3,2,1,0:T(8,128)S(1)}, u32[]{:S(2)}, u32[]{:S(2)}) collective-permute-start(f32[1,1,16,384]{3,2,1,0:T(8,128)S(1)} %get-tuple-element.104), channel_id=1, source_target_pairs={{0,4},{1,5},{2,6},{3,7},{8,12},{9,13},{10,14},{11,15},{16,20},{17,... | collective-permute-start | bytes 73736 | tf_op jit(solution)/shard_map/ppermute | solution.py:16
  46.0 4.6 %collective-permute-start.5 = (f32[1,1,16,384]{3,2,1,0:T(8,128)S(1)}, f32[1,1,16,384]{3,2,1,0:T(8,128)S(1)}, u32[]{:S(2)}, u32[]{:S(2)}) collective-permute-start(f32[1,1,16,384]{3,2,1,0:T(8,128)S(1)} %get-tuple-element.105), channel_id=1, source_target_pairs={{4,0},{5,1},{6,2},{7,3},{12,8},{13,9},{14,10},{15,11},{20,16},{21,... | collective-permute-start | bytes 73736 | tf_op jit(solution)/shard_map/ppermute | solution.py:19
  53.2 4.1 %collective-permute-start.6 = (f32[1,1,16,384]{3,2,1,0:T(8,128)S(1)}, f32[1,1,16,384]{3,2,1,0:T(8,128)S(1)}, u32[]{:S(2)}, u32[]{:S(2)}) collective-permute-start(f32[1,1,16,384]{3,2,1,0:T(8,128)S(1)} %get-tuple-element.102), channel_id=1, source_target_pairs={{0,4},{1,5},{2,6},{3,7},{8,12},{9,13},{10,14},{11,15},{16,20},{17,... | collective-permute-start | bytes 73736 | tf_op jit(solution)/shard_map/ppermute | solution.py:16
  54.8 4.6 %collective-permute-start.7 = (f32[1,1,16,384]{3,2,1,0:T(8,128)S(1)}, f32[1,1,16,384]{3,2,1,0:T(8,128)S(1)}, u32[]{:S(2)}, u32[]{:S(2)}) collective-permute-start(f32[1,1,16,384]{3,2,1,0:T(8,128)S(1)} %get-tuple-element.103), channel_id=1, source_target_pairs={{4,0},{5,1},{6,2},{7,3},{12,8},{13,9},{14,10},{15,11},{20,16},{21,... | collective-permute-start | bytes 73736 | tf_op jit(solution)/shard_map/ppermute | solution.py:19
  61.6 11.2 %copy-start.32 = (f32[1,1,8,16,256]{4,3,2,1,0:T(8,128)S(1)}, f32[1,1,8,16,256]{4,3,2,1,0:T(8,128)}, u32[]{:S(2)}) copy-start(f32[1,1,8,16,256]{4,3,2,1,0:T(8,128)} %param.7) | copy-start | bytes 393220
  61.7 11.3 %copy-start.30 = (f32[2,1,8,16,256]{4,3,2,1,0:T(8,128)S(1)}, f32[2,1,8,16,256]{4,3,2,1,0:T(8,128)}, u32[]{:S(2)}) copy-start(f32[2,1,8,16,256]{4,3,2,1,0:T(8,128)} %param.6) | copy-start | bytes 786436
  62.4 10.5 %collective-permute-start.8 = (f32[1,8,16,256]{3,2,1,0:T(8,128)S(1)}, f32[1,8,16,256]{3,2,1,0:T(8,128)S(1)}, u32[]{:S(2)}, u32[]{:S(2)}) collective-permute-start(f32[1,8,16,256]{3,2,1,0:T(8,128)S(1)} %maximum_select_fusion.3), channel_id=1, source_target_pairs={{0,8},{8,16},{16,24},{1,9},{9,17},{17,25},{2,10},{10,18},{18,26},{... | collective-permute-start | bytes 393224 | tf_op jit(solution)/shard_map/ppermute | solution.py:27
  71.0 7.7 %collective-permute-start.9 = (f32[2,1,8,16,256]{4,3,2,1,0:T(8,128)S(1)}, f32[2,1,8,16,256]{4,3,2,1,0:T(8,128)S(1)}, u32[]{:S(2)}, u32[]{:S(2)}) collective-permute-start(f32[2,1,8,16,256]{4,3,2,1,0:T(8,128)S(1)} %pad_maximum_fusion), channel_id=1, source_target_pairs={{8,0},{16,8},{24,16},{9,1},{17,9},{25,17},{10,2},{18,10},{26,18},{... | collective-permute-start | bytes 786440 | tf_op jit(solution)/shard_map/ppermute | solution.py:27
  78.8 2.7 %collective-permute-start.10 = (f32[1,1,16,384]{3,2,1,0:T(8,128)S(1)}, f32[1,1,16,384]{3,2,1,0:T(8,128)S(1)}, u32[]{:S(2)}, u32[]{:S(2)}) collective-permute-start(f32[1,1,16,384]{3,2,1,0:T(8,128)S(1)} %get-tuple-element.100), channel_id=1, source_target_pairs={{0,4},{1,5},{2,6},{3,7},{8,12},{9,13},{10,14},{11,15},{16,20},{17,... | collective-permute-start | bytes 73736 | tf_op jit(solution)/shard_map/ppermute | solution.py:16
  80.1 4.6 %collective-permute-start.11 = (f32[1,1,16,384]{3,2,1,0:T(8,128)S(1)}, f32[1,1,16,384]{3,2,1,0:T(8,128)S(1)}, u32[]{:S(2)}, u32[]{:S(2)}) collective-permute-start(f32[1,1,16,384]{3,2,1,0:T(8,128)S(1)} %get-tuple-element.101), channel_id=1, source_target_pairs={{4,0},{5,1},{6,2},{7,3},{12,8},{13,9},{14,10},{15,11},{20,16},{21,... | collective-permute-start | bytes 73736 | tf_op jit(solution)/shard_map/ppermute | solution.py:19
  87.9 4.3 %collective-permute-start.12 = (f32[1,1,16,384]{3,2,1,0:T(8,128)S(1)}, f32[1,1,16,384]{3,2,1,0:T(8,128)S(1)}, u32[]{:S(2)}, u32[]{:S(2)}) collective-permute-start(f32[1,1,16,384]{3,2,1,0:T(8,128)S(1)} %get-tuple-element.98), channel_id=1, source_target_pairs={{0,4},{1,5},{2,6},{3,7},{8,12},{9,13},{10,14},{11,15},{16,20},{17,... | collective-permute-start | bytes 73736 | tf_op jit(solution)/shard_map/ppermute | solution.py:16
  89.6 4.6 %collective-permute-start.13 = (f32[1,1,16,384]{3,2,1,0:T(8,128)S(1)}, f32[1,1,16,384]{3,2,1,0:T(8,128)S(1)}, u32[]{:S(2)}, u32[]{:S(2)}) collective-permute-start(f32[1,1,16,384]{3,2,1,0:T(8,128)S(1)} %get-tuple-element.99), channel_id=1, source_target_pairs={{4,0},{5,1},{6,2},{7,3},{12,8},{13,9},{14,10},{15,11},{20,16},{21,... | collective-permute-start | bytes 73736 | tf_op jit(solution)/shard_map/ppermute | solution.py:19
  97.1 7.7 %copy-start.20 = (f32[1,8,16,128]{3,2,1,0:T(8,128)}, f32[1,8,16,128]{3,2,1,0:T(8,128)S(1)}, u32[]{:S(2)}) copy-start(f32[1,8,16,128]{3,2,1,0:T(8,128)S(1)} %get-tuple-element.123) | copy-start | bytes 196612
  97.9 8.7 %copy-start.11 = (f32[1,8,16,256]{3,2,1,0:T(8,128)}, f32[1,8,16,256]{3,2,1,0:T(8,128)S(1)}, u32[]{:S(2)}) copy-start(f32[1,8,16,256]{3,2,1,0:T(8,128)S(1)} %get-tuple-element.12) | copy-start | bytes 393220
  97.9 12.6 %copy-start.15 = (f32[1,8,16,256]{3,2,1,0:T(8,128)}, f32[1,8,16,256]{3,2,1,0:T(8,128)S(1)}, u32[]{:S(2)}) copy-start(f32[1,8,16,256]{3,2,1,0:T(8,128)S(1)} %get-tuple-element.13) | copy-start | bytes 393220
  98.0 3.5 %collective-permute-start.14 = (f32[1,1,16,384]{3,2,1,0:T(8,128)S(1)}, f32[1,1,16,384]{3,2,1,0:T(8,128)S(1)}, u32[]{:S(2)}, u32[]{:S(2)}) collective-permute-start(f32[1,1,16,384]{3,2,1,0:T(8,128)S(1)} %get-tuple-element.96), channel_id=1, source_target_pairs={{0,4},{1,5},{2,6},{3,7},{8,12},{9,13},{10,14},{11,15},{16,20},{17,... | collective-permute-start | bytes 73736 | tf_op jit(solution)/shard_map/ppermute | solution.py:16
  100.1 4.6 %collective-permute-start.15 = (f32[1,1,16,384]{3,2,1,0:T(8,128)S(1)}, f32[1,1,16,384]{3,2,1,0:T(8,128)S(1)}, u32[]{:S(2)}, u32[]{:S(2)}) collective-permute-start(f32[1,1,16,384]{3,2,1,0:T(8,128)S(1)} %get-tuple-element.97), channel_id=1, source_target_pairs={{4,0},{5,1},{6,2},{7,3},{12,8},{13,9},{14,10},{15,11},{20,16},{21,... | collective-permute-start | bytes 73736 | tf_op jit(solution)/shard_map/ppermute | solution.py:19
  105.8 8.0 %copy-start.28 = (f32[1,8,16,128]{3,2,1,0:T(8,128)}, f32[1,8,16,128]{3,2,1,0:T(8,128)S(1)}, u32[]{:S(2)}) copy-start(f32[1,8,16,128]{3,2,1,0:T(8,128)S(1)} %get-tuple-element.127) | copy-start | bytes 196612
  106.5 7.3 %copy-start.22 = (f32[1,8,16,128]{3,2,1,0:T(8,128)}, f32[1,8,16,128]{3,2,1,0:T(8,128)S(1)}, u32[]{:S(2)}) copy-start(f32[1,8,16,128]{3,2,1,0:T(8,128)S(1)} %get-tuple-element.125) | copy-start | bytes 196612
  107.3 6.7 %copy-start.3 = (f32[1,8,16,128]{3,2,1,0:T(8,128)}, f32[1,8,16,128]{3,2,1,0:T(8,128)S(1)}, u32[]{:S(2)}) copy-start(f32[1,8,16,128]{3,2,1,0:T(8,128)S(1)} %slice_add_fusion) | copy-start | bytes 196612
  107.3 4.3 %collective-permute-start.16 = (f32[1,1,16,384]{3,2,1,0:T(8,128)S(1)}, f32[1,1,16,384]{3,2,1,0:T(8,128)S(1)}, u32[]{:S(2)}, u32[]{:S(2)}) collective-permute-start(f32[1,1,16,384]{3,2,1,0:T(8,128)S(1)} %get-tuple-element.94), channel_id=1, source_target_pairs={{0,4},{1,5},{2,6},{3,7},{8,12},{9,13},{10,14},{11,15},{16,20},{17,... | collective-permute-start | bytes 73736 | tf_op jit(solution)/shard_map/ppermute | solution.py:16
  109.0 4.6 %collective-permute-start.17 = (f32[1,1,16,384]{3,2,1,0:T(8,128)S(1)}, f32[1,1,16,384]{3,2,1,0:T(8,128)S(1)}, u32[]{:S(2)}, u32[]{:S(2)}) collective-permute-start(f32[1,1,16,384]{3,2,1,0:T(8,128)S(1)} %get-tuple-element.95), channel_id=1, source_target_pairs={{4,0},{5,1},{6,2},{7,3},{12,8},{13,9},{14,10},{15,11},{20,16},{21,... | collective-permute-start | bytes 73736 | tf_op jit(solution)/shard_map/ppermute | solution.py:19
  114.0 0.8 copy-start.24
  114.0 1.0 copy-start.27
  115.0 0.8 copy-start.26
  118.6 1.4 copy-start.16
  118.6 3.2 %copy-start.4 = (f32[1,8,16,128]{3,2,1,0:T(8,128)S(1)}, f32[1,8,16,128]{3,2,1,0:T(8,128)}, u32[]{:S(2)}) copy-start(f32[1,8,16,128]{3,2,1,0:T(8,128)} %copy-done.3) | copy-start | bytes 196612
  118.7 3.2 %copy-start.12 = (f32[1,8,16,256]{3,2,1,0:T(8,128)S(1)}, f32[1,8,16,256]{3,2,1,0:T(8,128)}, u32[]{:S(2)}) copy-start(f32[1,8,16,256]{3,2,1,0:T(8,128)} %copy-done.11) | copy-start | bytes 393220
  118.7 5.0 %copy-start.21 = (f32[1,8,16,128]{3,2,1,0:T(8,128)S(1)}, f32[1,8,16,128]{3,2,1,0:T(8,128)}, u32[]{:S(2)}) copy-start(f32[1,8,16,128]{3,2,1,0:T(8,128)} %copy-done.20) | copy-start | bytes 196612
  118.7 4.9 %copy-start.23 = (f32[1,8,16,128]{3,2,1,0:T(8,128)S(1)}, f32[1,8,16,128]{3,2,1,0:T(8,128)}, u32[]{:S(2)}) copy-start(f32[1,8,16,128]{3,2,1,0:T(8,128)} %copy-done.22) | copy-start | bytes 196612
  119.4 5.0 %copy-start.29 = (f32[1,8,16,128]{3,2,1,0:T(8,128)S(1)}, f32[1,8,16,128]{3,2,1,0:T(8,128)}, u32[]{:S(2)}) copy-start(f32[1,8,16,128]{3,2,1,0:T(8,128)} %copy-done.28) | copy-start | bytes 196612
  119.4 5.0 %copy-start.31 = (f32[1,1,8,16,128]{4,3,2,1,0:T(8,128)S(1)}, f32[1,1,8,16,128]{4,3,2,1,0:T(8,128)}, u32[]{:S(2)}) copy-start(f32[1,1,8,16,128]{4,3,2,1,0:T(8,128)} %get-tuple-element.92) | copy-start | bytes 196612
  120.0 3.7 %copy-start.25 = (f32[1,8,16,1152]{3,2,1,0:T(8,128)S(1)}, f32[1,8,16,1152]{3,2,1,0:T(8,128)}, u32[]{:S(2)}) copy-start(f32[1,8,16,1152]{3,2,1,0:T(8,128)} %constant_dynamic-update-slice_fusion.198) | copy-start | bytes 1769476
Sparse Core Ops, SparseCore 0:
  118.8 70.7 reduce-scatter.1
where the time goes:
time: 201 us; the launch traced here: 198 us
  waiting for transfers between devices  86.9 us (43%)
  starting transfers between devices  40 us (20%)
  matrix products  29.4 us (15%)
  between operations  17.3 us (9%)
  other arithmetic  13.7 us (7%)
  local copies, waits for them, and re-layouts  10.9 us (5%)
    reduce_scatter x1, waiting for transfers between devices, per_device(): lax.psum_scatter(running, ('row', 'dp'), scatter_dimension=2, tiled=True)  63.8 us
    dot_general x24, matrix products, matmul(): jnp.dot(left, right, precision=HIGHEST, preferred_element_type=jnp.float32)  20.6 us
    ppermute x8, starting transfers between devices, with_halo(): lax.ppermute(lax.slice_in_dim(block, block.shape[dim] - width, None, axis...  19.3 us
    ppermute x8, waiting for transfers between devices, with_halo(): lax.ppermute(lax.slice_in_dim(block, 0, width, axis=dim), axis, backward)  17.5 us
    ppermute x8, starting transfers between devices, with_halo(): lax.ppermute(lax.slice_in_dim(block, 0, width, axis=dim), axis, backward)  11 us
    ppermute x2, starting transfers between devices, from_behind(): return lax.ppermute(value, axis, pairs)  9.68 us
    dot_general x8, matrix products, pullback(): lax.dot_general(patches, cotangent.reshape(-1, cotangent.shape[-1]), (((0...  8.76 us
    ppermute x2, waiting for transfers between devices, from_behind(): return lax.ppermute(value, axis, pairs)  5.64 us
  transfers between devices with their start and end apart: 19, of which 9 were waited for; matrix products, arithmetic and copies ran while one was open for 9% of the time, Pallas kernels for 0%

commit v1 on v0

v1 whole, which is shorter than its diff:
```python
import functools
import math

import jax
import jax.numpy as jnp
from jax import lax
from jax.experimental import pallas as pl
from jax.experimental.pallas import tpu as pltpu
from jax.sharding import PartitionSpec as P

MESH = pl.DeviceIdType.MESH
SRC, OUT, GRAD = 0, 1, 2


def split_float(value):
    high = value.astype(jnp.bfloat16)
    low = (value - high.astype(jnp.float32)).astype(jnp.bfloat16)
    return high, low


def kernel_body(
    sizes,
    fresh,
    target,
    carried,
    returning,
    weights,
    blocks,
    grads_out,
    leaving,
    sent_back,
    st,
    produced,
    aims,
    keep,
    w_fwd,
    w_flip,
    pad_fwd,
    pad_src,
    pad_cot,
    src_t,
    sums,
    landed,
    row_send,
    row_recv,
    late_send,
    late_recv,
    seg_send,
    seg_recv,
    red_send,
    red_recv,
):
    ticks, seg_n, row_n, dp_n, width, local, chans, taps, reach, scale = sizes
    cells = local * row_n
    levels = dp_n.bit_length() - 1
    chunk = (9 * chans) // (row_n * dp_n)
    seg = lax.axis_index("segment")
    row = lax.axis_index("row")
    dp = lax.axis_index("dp")
    not_first = seg > 0
    not_last = seg < seg_n - 1

    barrier = pltpu.get_barrier_semaphore()
    row_peers = [lax.rem(row + k, row_n) for k in range(1, row_n)]
    dp_peers = [
        dp + (1 << lev) - 2 * (1 << lev) * lax.rem(dp // (1 << lev), 2) for lev in range(levels)
    ]
    for peer in row_peers:
        pl.semaphore_signal(barrier, inc=1, device_id={"row": peer}, device_id_type=MESH)
    for peer in dp_peers:
        pl.semaphore_signal(barrier, inc=1, device_id={"dp": peer}, device_id_type=MESH)

    @pl.when(not_first)
    def _():
        pl.semaphore_signal(barrier, inc=1, device_id={"segment": seg - 1}, device_id_type=MESH)

    @pl.when(not_last)
    def _():
        pl.semaphore_signal(barrier, inc=1, device_id={"segment": seg + 1}, device_id_type=MESH)

    always = len(row_peers) + len(dp_peers)
    pl.semaphore_wait(barrier, always + not_first.astype(jnp.int32) + not_last.astype(jnp.int32))

    mine = pl.ds(pl.multiple_of(row * local, local), local)

    def lanes(half):
        return slice(half * chans, (half + 1) * chans)

    order = [(SRC, 1), (OUT, 0), (GRAD, 1), (SRC, 0), (OUT, 1), (GRAD, 0)]

    def row_copy(place, k, ref, send, recv):
        return pltpu.make_async_remote_copy(
            src_ref=ref,
            dst_ref=ref,
            send_sem=send.at[place, k],
            recv_sem=recv.at[place, k],
            device_id={"row": row_peers[k]},
            device_id_type=MESH,
        )

    def gathers(place):
        field, half = order[place]
        return [
            row_copy(place, k, st.at[0, field, half, mine], row_send, row_recv)
            for k in range(row_n - 1)
        ]

    for place, (field, half) in enumerate(order):
        if field == SRC:
            first = jnp.full((local, chans), seg, jnp.int32) == 0
            value = jnp.where(first, fresh[0, :, lanes(half)], carried[:, lanes(half)])
        else:
            value = returning[field - 1, :, lanes(half)]
        st[0, field, half, mine] = value
        for copy in gathers(place):
            copy.start()

    def fresh_copies():
        return [
            row_copy(2 * tick + half - 2, k, st.at[tick, SRC, half, mine], late_send, late_recv)
            for tick in range(1, ticks)
            for half in range(2)
            for k in range(row_n - 1)
        ]

    def target_copies():
        return [
            row_copy(2 * tick + half, k, aims.at[tick, half, mine], late_send, late_recv)
            for tick in range(ticks - 1)
            for half in range(2)
            for k in range(row_n - 1)
        ]

    @pl.when(seg == 0)
    def _():
        for tick in range(1, ticks):
            for half in range(2):
                st[tick, SRC, half, mine] = fresh[tick, :, lanes(half)]
        for copy in fresh_copies():
            copy.start()

    @pl.when(seg == seg_n - 1)
    def _():
        for tick in range(ticks - 1):
            for half in range(2):
                aims[tick, half, mine] = target[tick, :, lanes(half)]
        for copy in target_copies():
            copy.start()

    def store_kernel(ref, pair, tap, value):
        high, low = split_float(value)
        base = tap * (2 * chans)
        for part in range(2):
            rows = pl.ds(pl.multiple_of(base + part * chans, chans), chans)
            ref[pair, rows, :chans] = high
            ref[pair, rows, chans:] = low

    def prepare(index, carry):
        pair = index // 9
        tap = index - 9 * pair
        value = weights[pair, pl.ds(pl.multiple_of(tap * chans, chans), chans), :]
        store_kernel(w_fwd, pair, tap, value)
        store_kernel(w_flip, pair, 8 - tap, value.T)
        return carry

    lax.fori_loop(0, 36, prepare, 0)

    rim = jnp.zeros((width, 2 * chans), jnp.bfloat16)
    for side in range(3):
        for start in (0, width + cells):
            pad_fwd[side, start : start + width] = rim
            pad_src[side, start : start + width] = rim
            for slot in range(4):
                pad_cot[slot, side, start : start + width] = rim

    column = lax.rem(lax.broadcasted_iota(jnp.int32, (cells, chans), 0), width)

    def fill(view, value):
        before = jnp.where(column == 0, 0.0, pltpu.roll(value, 1, 0))
        after = jnp.where(column == width - 1, 0.0, pltpu.roll(value, cells - 1, 0))
        for side, shifted in enumerate((before, value, after)):
            high, low = split_float(shifted)
            view[side, width : width + cells, :chans] = high
            view[side, width : width + cells, chans:] = low

    def conv(view, kernel):
        patches = jnp.concatenate(
            [
                view[tap % 3, (tap // 3) * width : (tap // 3) * width + cells, :]
                for tap in range(9)
            ],
            axis=1,
        )
        both = jnp.dot(patches, kernel, preferred_element_type=jnp.float32)
        return both[:, :chans] + both[:, chans:]

    doubled = jnp.full((cells, chans), blocks[0], jnp.int32) == 2

    def pair_of(step):
        return 2 * (1 - step // 2) + 1 - step % 2

    def forward_step(tick, step):
        even = step % 2 == 0
        source, goal = (1, 0) if even else (0, 1)
        held = st if step < 2 else keep
        if step == 0:
            value = st[tick, SRC, source]
        elif step == 1:
            value = keep[source]
        else:
            value = keep[source]
        fill(pad_fwd, jax.nn.silu(value))
        base = st[tick, SRC, goal] if step < 2 else keep[goal]
        fresh_value = base + conv(pad_fwd, w_fwd[step])
        if step < 2:
            keep[goal] = fresh_value
        else:
            chosen = jnp.where(doubled, fresh_value, keep[goal])
            keep[goal] = fresh_value
            produced[tick, SRC, goal] = chosen

    def backward_open(tick, step):
        even = step % 2 == 0
        held = (lambda f, h: st[tick, f, h]) if step == 0 else (lambda f, h: produced[tick, f, h])
        if step == 0:
            source, cot = st[tick, OUT, 0], st[tick, GRAD, 1]
        elif even:
            source, cot = produced[tick, OUT, 0], produced[tick, GRAD, 1]
        else:
            source, cot = produced[tick, OUT, 1], produced[tick, GRAD, 0]
        if step == 1:
            source, cot = produced[tick, OUT, 1], produced[tick, GRAD, 0]
        logistic = jax.nn.sigmoid(source)
        active = source * logistic
        fill(pad_src, active)
        fill(pad_cot.at[step], cot)
        high, low = split_float(active.T)
        src_t[step, :chans] = high
        src_t[step, chans:] = low
        return logistic * (1.0 + source * (1.0 - logistic))

    def backward_close(tick, step, slope):
        even = step % 2 == 0
        out_goal, grad_goal = (1, 0) if even else (0, 1)
        holder = st if step < 2 else produced
        out_old = holder[tick, OUT, out_goal]
        grad_old = holder[tick, GRAD, grad_goal]
        rebuilt = conv(pad_src, w_fwd[pair_of(step)])
        added = conv(pad_cot.at[step], w_flip[pair_of(step)]) * slope
        out_new = out_old - rebuilt
        grad_new = grad_old + added
        produced[tick, OUT, out_goal] = out_new
        produced[tick, GRAD, grad_goal] = grad_new
        if step == 1:
            for half in range(2):
                for field in (OUT, GRAD):
                    produced[tick, field, half] = jnp.where(
                        doubled, produced[tick, field, half], st[tick, field, half]
                    )

    first_tap = jnp.minimum((row * (9 * chans // row_n)) // chans, 9 - taps)

    def kernel_grads(tick, step):
        pair = pair_of(step)
        for extra in range(taps):
            other = 8 - first_tap - extra
            down = other // 3
            side = other - 3 * down
            cots = pad_cot[step, side, pl.ds(pl.multiple_of(down * width, width), cells), :]
            four = jnp.dot(src_t[step], cots, preferred_element_type=jnp.float32)
            two = four[:chans] + four[chans:]
            value = two[:, :chans] + two[:, chans:]
            rows = slice(extra * chans, (extra + 1) * chans)
            if tick > 0:
                value = value + sums[pair, rows]
            sums[pair, rows] = value

    def seg_copy(tick, field, half):
        by = 1 if field == SRC else -1
        slot = (tick * 3 + field) * 2 + half

        def make(to):
            return pltpu.make_async_remote_copy(
                src_ref=produced.at[tick, field, half],
                dst_ref=st.at[tick + 1, field, half],
                send_sem=seg_send.at[slot],
                recv_sem=seg_recv.at[slot],
                device_id={"segment": to},
                device_id_type=MESH,
            )

        return make, by

    def seg_start(tick, field, half):
        make, by = seg_copy(tick, field, half)

        @pl.when(not_last if by > 0 else not_first)
        def _():
            make(seg + by).start()

    def seg_wait_recv(tick, field, half):
        make, by = seg_copy(tick, field, half)

        @pl.when(not_first if by > 0 else not_last)
        def _():
            make(seg - by).wait_recv()

    def seg_wait_send(tick, field, half):
        make, by = seg_copy(tick, field, half)

        @pl.when(not_last if by > 0 else not_first)
        def _():
            make(seg + by).wait_send()

    offset = row * (9 * chans // row_n) - first_tap * chans

    def chunk_rows(index):
        return pl.ds(pl.multiple_of(offset + index * chunk, 16), chunk)

    def red_places(level):
        span = 1 << (level + 1)
        count = dp_n // span
        start = sum(dp_n >> (lev + 1) for lev in range(level))
        return span, count, start

    def red_copies(pair, level):
        span, count, start = red_places(level)
        away = lax.rem(dp_peers[level], span)
        return [
            pltpu.make_async_remote_copy(
                src_ref=sums.at[pair, chunk_rows(away + span * j)],
                dst_ref=landed.at[pair, start + j],
                send_sem=red_send.at[pair, start + j],
                recv_sem=red_recv.at[pair, start + j],
                device_id={"dp": dp_peers[level]},
                device_id_type=MESH,
            )
            for j in range(count)
        ]

    def red_start(pair, level):
        if level < levels:
            for copy in red_copies(pair, level):
                copy.start()

    def red_finish(pair, level):
        span, count, start = red_places(level)
        own = lax.rem(dp, span)
        for j, copy in enumerate(red_copies(pair, level)):
            copy.wait_recv()
            rows = chunk_rows(own + span * j)
            sums[pair, rows] = sums[pair, rows] + landed[pair, start + j]

    for tick in range(ticks):
        final = tick == ticks - 1
        for step in range(4):
            if tick == 0:
                if step == 0:
                    for place in range(3):
                        for copy in gathers(place):
                            copy.wait_recv()
            elif step == 0:
                seg_wait_recv(tick - 1, OUT, 0)
                seg_wait_recv(tick - 1, GRAD, 1)
            slope = backward_open(tick, step)
            if final:
                kernel_grads(tick, step)
                red_start(pair_of(step), 0)
            if step == 0:
                if tick == 0:
                    for place in range(3, 6):
                        for copy in gathers(place):
                            copy.wait_recv()
                else:
                    seg_wait_recv(tick - 1, OUT, 1)
                    seg_wait_recv(tick - 1, GRAD, 0)
            if not final:
                if step == 0 and tick > 0:
                    seg_wait_recv(tick - 1, SRC, 0)
                    seg_wait_recv(tick - 1, SRC, 1)
                forward_step(tick, step)
            backward_close(tick, step, slope)
            if not final and step >= 2:
                even = step % 2 == 0
                seg_start(tick, SRC, 0 if even else 1)
                seg_start(tick, OUT, 1 if even else 0)
                seg_start(tick, GRAD, 0 if even else 1)
        if not final:
            if tick == 0:

                @pl.when(seg == 0)
                def _():
                    for copy in fresh_copies():
                        copy.wait_recv()

                @pl.when(seg == seg_n - 1)
                def _():
                    for copy in target_copies():
                        copy.wait_recv()

            @pl.when(seg == seg_n - 1)
            def _(tick=tick):
                for half in range(2):
                    value = produced[tick, SRC, half]
                    st[tick + 1, OUT, half] = value
                    st[tick + 1, GRAD, half] = value - aims[tick, half]

            for step in range(4):
                kernel_grads(tick, step)
        else:
            if tick > 0:
                seg_wait_recv(tick - 1, SRC, 0)
                seg_wait_recv(tick - 1, SRC, 1)
            for step in range(4):
                if levels > 0:
                    red_finish(pair_of(step), 0)
                    red_start(pair_of(step), 1)
                forward_step(tick, step)

    last = ticks - 1
    for half in range(2):
        leaving[:, lanes(half)] = produced[last, SRC, half, mine]
        for field in (OUT, GRAD):
            sent_back[field - 1, :, lanes(half)] = produced[last, field, half, mine]

    for level in range(1, levels):
        for step in range(4):
            red_finish(pair_of(step), level)
            red_start(pair_of(step), level + 1)
    twice = jnp.full((chunk, chans), blocks[0], jnp.int32) == 2
    for pair in range(4):
        total = sums[pair, chunk_rows(dp)] * scale
        if pair >= 2:
            total = jnp.where(twice, total, 0.0)
        grads_out[pair] = total

    for place in range(6):
        for copy in gathers(place):
            copy.wait_send()

    @pl.when(seg == 0)
    def _():
        for copy in fresh_copies():
            copy.wait_send()

    @pl.when(seg == seg_n - 1)
    def _():
        for copy in target_copies():
            copy.wait_send()

    for tick in range(ticks - 1):
        for field in (SRC, OUT, GRAD):
            for half in range(2):
                seg_wait_send(tick, field, half)
    for level in range(levels):
        for pair in range(4):
            for copy in red_copies(pair, level):
                copy.wait_send()


def per_device(axis_sizes, fresh, target, carried, returning, weights, section_blocks):
    seg_n, row_n, dp_n = axis_sizes
    ticks, crops, rows_here, width, both = fresh.shape
    assert crops == 1 and dp_n & (dp_n - 1) == 0
    chans = both // 2
    local = rows_here * width
    cells = local * row_n
    held = 9 * chans // row_n
    taps = max(-(-(r + 1) * held // chans) - r * held // chans for r in range(row_n))
    reach = dp_n - 1
    chunk = held // dp_n
    scale = 1.0 / math.sqrt(ticks * dp_n * cells)
    sizes = (ticks, seg_n, row_n, dp_n, width, local, chans, taps, reach, scale)
    pairs = 4
    f32, b16 = jnp.float32, jnp.bfloat16
    padded = cells + 2 * width
    dma = pltpu.SemaphoreType.DMA
    peers = max(row_n - 1, 1)
    late = 2 * max(ticks - 1, 1)
    vmem = pl.BlockSpec(memory_space=pltpu.VMEM)
    flops = ticks * 4 * (3 * 9 + taps) * 2 * cells * chans * chans * 4
    grads_out, leaving, sent_back = pl.pallas_call(
        functools.partial(kernel_body, sizes),
        out_shape=(
            jax.ShapeDtypeStruct((pairs, chunk, chans), f32),
            jax.ShapeDtypeStruct((local, both), f32),
            jax.ShapeDtypeStruct((2, local, both), f32),
        ),
        in_specs=[vmem] * 5 + [pl.BlockSpec(memory_space=pltpu.SMEM)],
        out_specs=(vmem, vmem, vmem),
        scratch_shapes=[
            pltpu.VMEM((ticks, 3, 2, cells, chans), f32),
            pltpu.VMEM((ticks, 3, 2, cells, chans), f32),
            pltpu.VMEM((max(ticks - 1, 1), 2, cells, chans), f32),
            pltpu.VMEM((2, cells, chans), f32),
            pltpu.VMEM((pairs, 18 * chans, 2 * chans), b16),
            pltpu.VMEM((pairs, 18 * chans, 2 * chans), b16),
            pltpu.VMEM((3, padded, 2 * chans), b16),
            pltpu.VMEM((3, padded, 2 * chans), b16),
            pltpu.VMEM((4, 3, padded, 2 * chans), b16),
            pltpu.VMEM((4, 2 * chans, cells), b16),
            pltpu.VMEM((pairs, taps * chans, chans), f32),
            pltpu.VMEM((pairs, max(reach, 1), chunk, chans), f32),
            dma((6, peers)),
            dma((6, peers)),
            dma((late, peers)),
            dma((late, peers)),
            dma((6 * ticks,)),
            dma((6 * ticks,)),
            dma((pairs, max(reach, 1))),
            dma((pairs, max(reach, 1))),
        ],
        cost_estimate=pl.CostEstimate(flops=flops, bytes_accessed=1 << 22, transcendentals=1 << 20),
        compiler_params=pltpu.CompilerParams(
            collective_id=0, has_side_effects=True, vmem_limit_bytes=48 << 20
        ),
    )(
        fresh.reshape(ticks, local, both),
        target.reshape(-1, local, both),
        carried.reshape(local, both),
        returning.reshape(2, local, both),
        weights.reshape(pairs, 9 * chans, chans),
        section_blocks,
    )
    return (
        grads_out.reshape(1, 2, 2, chunk, chans),
        leaving.reshape(1, 1, rows_here, width, both),
        sent_back.reshape(1, 2, 1, rows_here, width, both),
    )


def solution(mesh):
    axis_sizes = (mesh.shape["segment"], mesh.shape["row"], mesh.shape["dp"])
    return jax.shard_map(
        functools.partial(per_device, axis_sizes),
        mesh=mesh,
        in_specs=(
            P(None, "dp", "row", None, None),
            P(None, "dp", "row", None, None),
            P("segment", "dp", "row", None, None),
            P("segment", None, "dp", "row", None, None),
            P("segment", None, None, None, None),
            P("segment"),
        ),
        out_specs=(
            P("segment", None, None, ("row", "dp"), None),
            P("segment", "dp", "row", None, None),
            P("segment", None, "dp", "row", None, None),
        ),
        check_vma=False,
    )
```

time: 201 us -> 54.5 us (0.27); the launches traced: 198 us -> 54.3 us
  waiting for transfers between devices: 86.9 us -> 0 us
  Pallas kernels: 0 us -> 45.5 us
  starting transfers between devices: 40 us -> 0 us
  matrix products: 29.4 us -> 0 us
  between operations: 17.3 us -> 1.3 us
  other arithmetic: 13.7 us -> 0 us
  local copies, waits for them, and re-layouts: 10.9 us -> 7.44 us
    reduce_scatter x1 -> x0, waiting for transfers between devices: 63.8 us -> none  [per_device(): lax.psum_scatter(running, ('row', 'dp'), scatter_dimension=2, tiled=True)]
    pallas_call x0 -> x1, Pallas kernels: none -> 45.5 us  [per_device(): pl.pallas_call(functools.partial(kernel_body, sizes), out_shape=(jax.Shap...]
    ppermute x18 -> x0, starting transfers between devices: 39.9 us -> none  [the longest x8 19.3 us: with_halo(): lax.ppermute(lax.slice_in_dim(block, block.shape[dim] - width, None, axis...]
    dot_general x32 -> x0, matrix products: 29.4 us -> none  [the longest x24 20.6 us: matmul(): jnp.dot(left, right, precision=HIGHEST, preferred_element_type=jnp.float32)]
    ppermute x18 -> x0, waiting for transfers between devices: 23.1 us -> none  [the longest x8 17.5 us: with_halo(): lax.ppermute(lax.slice_in_dim(block, 0, width, axis=dim), axis, backward)]
    unnamed x32 -> x0, other arithmetic: 3.94 us -> none
    unnamed x194 -> x13, local copies, waits for them, and re-layouts: 3.66 us -> 7.44 us
    transpose x8 -> x0, local copies, waits for them, and re-layouts: 2.74 us -> none  [flipped(): return kernel.reshape(3, 3, chans, chans)[::-1, ::-1].transpose(0, 1, 3,...]
  transfers between devices with their start and end apart: 19 -> 0, of which waited for: 9 -> 0; matrix products, arithmetic and copies ran while one was open for 9% -> 0% of each run, Pallas kernels for 0% -> 0%
where the time goes in v1:
time: 54.5 us; the launch traced here: 54.3 us
  Pallas kernels  45.5 us (83%)
  local copies, waits for them, and re-layouts  7.44 us (14%)
  between operations  1.3 us (2%)
    pallas_call x1, Pallas kernels, per_device(): pl.pallas_call(functools.partial(kernel_body, sizes), out_shape=(jax.Shap...  45.5 us
    unnamed x13, local copies, waits for them, and re-layouts  7.44 us

profile of v1, /device:TPU:1, one launch (start us, length us, event | category | flops | bytes accessed | tf_op | source)
XLA Modules:
  0.0 54.3 jit_solution(5712249362279922491)
XLA Ops:
  1.3 0.0 copy-start
  1.3 1.7 %copy-done = f32[1,2,2,1152,128]{4,3,2,1,0:T(8,128)S(1)} copy-done((f32[1,2,2,1152,128]{4,3,2,1,0:T(8,128)S(1)}, f32[1,2,2,1152,128]{4,3,2,1,0:T(8,128)}, u32[]{:S(2)}) %copy-start) | copy-done | bytes 2359320
  2.9 0.0 copy-start.1
  2.9 0.9 %copy-done.1 = f32[2,1,8,16,256]{4,3,2,1,0:T(8,128)S(1)} copy-done((f32[2,1,8,16,256]{4,3,2,1,0:T(8,128)S(1)}, f32[2,1,8,16,256]{4,3,2,1,0:T(8,128)}, u32[]{:S(2)}) %copy-start.1) | copy-done | bytes 262168
  3.9 0.0 copy-start.2
  3.9 0.9 %copy-done.2 = f32[1,2,1,8,16,256]{5,4,3,2,1,0:T(8,128)S(1)} copy-done((f32[1,2,1,8,16,256]{5,4,3,2,1,0:T(8,128)S(1)}, f32[1,2,1,8,16,256]{5,4,3,2,1,0:T(8,128)}, u32[]{:S(2)}) %copy-start.2) | copy-done | bytes 262168
  4.8 0.0 copy-start.3
  4.8 0.9 %copy-done.3 = f32[1,1,8,16,256]{4,3,2,1,0:T(8,128)S(1)} copy-done((f32[1,1,8,16,256]{4,3,2,1,0:T(8,128)S(1)}, f32[1,1,8,16,256]{4,3,2,1,0:T(8,128)}, u32[]{:S(2)}) %copy-start.3) | copy-done | bytes 131096
  5.8 0.0 copy-start.4
  5.8 0.9 %copy-done.4 = f32[1,1,8,16,256]{4,3,2,1,0:T(8,128)S(1)} copy-done((f32[1,1,8,16,256]{4,3,2,1,0:T(8,128)S(1)}, f32[1,1,8,16,256]{4,3,2,1,0:T(8,128)}, u32[]{:S(2)}) %copy-start.4) | copy-done | bytes 131096
  6.7 45.5 %shard_map.85 = (f32[4,144,128]{2,1,0:T(8,128)S(1)}, f32[128,256]{1,0:T(8,128)S(1)}, f32[2,128,256]{2,1,0:T(8,128)S(1)}) custom-call(f32[2,128,256]{2,1,0:T(8,128)S(1)} %bitcast.14, f32[1,128,256]{2,1,0:T(8,128)S(1)} %bitcast.16, f32[128,256]{1,0:T(8,128)S(1)} %bitcast.17, f32[2,128,256]{2,1,0:T(8,128)S(1)} %bitcast.15, f32[4,1152,128]{2,1,0:T(8,128)S(1)} %bitcast.13, ...), custom_call_target="tpu_custom_call" | custom-call | flops 8589934592 | bytes 4194304 | tf_op jit(solution)/shard_map/pallas_call | solution.py:482
  52.2 0.7 %copy.14 = f32[1,2,2,144,128]{4,3,2,1,0:T(8,128)} copy(f32[1,2,2,144,128]{4,3,2,1,0:T(8,128)S(1)} %bitcast.10) | data formatting | bytes 589824
  52.9 0.7 %copy.15 = f32[1,1,8,16,256]{4,3,2,1,0:T(8,128)} copy(f32[1,1,8,16,256]{4,3,2,1,0:T(8,128)S(1)} %bitcast.12) | data formatting | bytes 262144
  53.6 0.7 %copy.16 = f32[1,2,1,8,16,256]{5,4,3,2,1,0:T(8,128)} copy(f32[1,2,1,8,16,256]{5,4,3,2,1,0:T(8,128)S(1)} %bitcast.11) | data formatting | bytes 524288
Async XLA Ops:
  1.3 1.7 %copy-start = (f32[1,2,2,1152,128]{4,3,2,1,0:T(8,128)S(1)}, f32[1,2,2,1152,128]{4,3,2,1,0:T(8,128)}, u32[]{:S(2)}) copy-start(f32[1,2,2,1152,128]{4,3,2,1,0:T(8,128)} %param.10) | copy-start | bytes 7077892
  2.9 0.9 %copy-start.1 = (f32[2,1,8,16,256]{4,3,2,1,0:T(8,128)S(1)}, f32[2,1,8,16,256]{4,3,2,1,0:T(8,128)}, u32[]{:S(2)}) copy-start(f32[2,1,8,16,256]{4,3,2,1,0:T(8,128)} %param.6) | copy-start | bytes 786436
  3.9 0.9 %copy-start.2 = (f32[1,2,1,8,16,256]{5,4,3,2,1,0:T(8,128)S(1)}, f32[1,2,1,8,16,256]{5,4,3,2,1,0:T(8,128)}, u32[]{:S(2)}) copy-start(f32[1,2,1,8,16,256]{5,4,3,2,1,0:T(8,128)} %param.9) | copy-start | bytes 786436
  4.8 0.9 %copy-start.3 = (f32[1,1,8,16,256]{4,3,2,1,0:T(8,128)S(1)}, f32[1,1,8,16,256]{4,3,2,1,0:T(8,128)}, u32[]{:S(2)}) copy-start(f32[1,1,8,16,256]{4,3,2,1,0:T(8,128)} %param.7) | copy-start | bytes 393220
  5.8 0.9 %copy-start.4 = (f32[1,1,8,16,256]{4,3,2,1,0:T(8,128)S(1)}, f32[1,1,8,16,256]{4,3,2,1,0:T(8,128)}, u32[]{:S(2)}) copy-start(f32[1,1,8,16,256]{4,3,2,1,0:T(8,128)} %param.8) | copy-start | bytes 393220

commit v2 on v1

--- a/solution.py
+++ b/solution.py
@@ -49,6 +49,10 @@
     seg_recv,
     red_send,
     red_recv,
+    held_weights,
+    own_sem,
+    late_sem,
+    weight_sem,
 ):
     ticks, seg_n, row_n, dp_n, width, local, chans, taps, reach, scale = sizes
     cells = local * row_n
@@ -78,74 +82,116 @@
     def _():
         pl.semaphore_signal(barrier, inc=1, device_id={"segment": seg + 1}, device_id_type=MESH)
 
+    mine = pl.ds(pl.multiple_of(row * local, local), local)
+
+    def lanes(half):
+        return slice(half * chans, (half + 1) * chans)
+
+    order = [(OUT, 0), (GRAD, 1), (OUT, 1), (GRAD, 0), (SRC, 1), (SRC, 0)]
+
+    def fresh_part(place):
+        field, half = order[place]
+        return fresh.at[0, :, lanes(half)]
+
+    def plain_part(place):
+        field, half = order[place]
+        if field == SRC:
+            return carried.at[:, lanes(half)]
+        return returning.at[field - 1, :, lanes(half)]
+
+    def own_copy(place, part):
+        field, half = order[place]
+        return pltpu.make_async_copy(part, st.at[0, field, half, mine], own_sem.at[place])
+
+    def row_copies(place, part, goal, send, recv):
+        return [
+            pltpu.make_async_remote_copy(
+                src_ref=part,
+                dst_ref=goal,
+                send_sem=send.at[place, k],
+                recv_sem=recv.at[place, k],
+                device_id={"row": row_peers[k]},
+                device_id_type=MESH,
+            )
+            for k in range(row_n - 1)
+        ]
+
+    def gathers(place, part):
+        field, half = order[place]
+        return row_copies(place, part, st.at[0, field, half, mine], row_send, row_recv)
+
+    def at_place(place, action):
+        if order[place][0] == SRC:
+
+            @pl.when(seg == 0)
+            def _():
+                action(fresh_part(place))
+
+            @pl.when(seg > 0)
+            def _():
+                action(plain_part(place))
+        else:
+            action(plain_part(place))
+
+    def each(copies, action):
+        for copy in copies:
+            action(copy)
+
+    weight_copy = pltpu.make_async_copy(weights, held_weights, weight_sem.at[0])
+    weight_copy.start()
+    for place in range(6):
+        at_place(place, lambda part: own_copy(place, part).start())
+
+    def late_parts(of_target):
+        parts = []
+        for tick in range(ticks - 1):
+            for half in range(2):
+                if of_target:
+                    parts.append((target.at[tick, :, lanes(half)], aims.at[tick, half, mine]))
+                else:
+                    parts.append(
+                        (fresh.at[tick + 1, :, lanes(half)], st.at[tick + 1, SRC, half, mine])
+                    )
+        return parts
+
+    def late_each(action):
+        for of_target, here in ((False, seg == 0), (True, seg == seg_n - 1)):
+
+            @pl.when(here)
+            def _(of_target=of_target):
+                for place, (part, goal) in enumerate(late_parts(of_target)):
+                    own = functools.partial(
+                        pltpu.make_async_copy, part, goal, late_sem.at[place]
+                    )
+                    action(own, row_copies(place, part, goal, late_send, late_recv))
+
     always = len(row_peers) + len(dp_peers)
     pl.semaphore_wait(barrier, always + not_first.astype(jnp.int32) + not_last.astype(jnp.int32))
 
-    mine = pl.ds(pl.multiple_of(row * local, local), local)
-
-    def lanes(half):
-        return slice(half * chans, (half + 1) * chans)
-
-    order = [(SRC, 1), (OUT, 0), (GRAD, 1), (SRC, 0), (OUT, 1), (GRAD, 0)]
-
-    def row_copy(place, k, ref, send, recv):
-        return pltpu.make_async_remote_copy(
-            src_ref=ref,
-            dst_ref=ref,
-            send_sem=send.at[place, k],
-            recv_sem=recv.at[place, k],
-            device_id={"row": row_peers[k]},
-            device_id_type=MESH,
-        )
-
-    def gathers(place):
-        field, half = order[place]
-        return [
-            row_copy(place, k, st.at[0, field, half, mine], row_send, row_recv)
-            for k in range(row_n - 1)
-        ]
-
-    for place, (field, half) in enumerate(order):
-        if field == SRC:
-            first = jnp.full((local, chans), seg, jnp.int32) == 0
-            value = jnp.where(first, fresh[0, :, lanes(half)], carried[:, lanes(half)])
-        else:
-            value = returning[field - 1, :, lanes(half)]
-        st[0, field, half, mine] = value
-        for copy in gathers(place):
-            copy.start()
-
-    def fresh_copies():
-        return [
-            row_copy(2 * tick + half - 2, k, st.at[tick, SRC, half, mine], late_send, late_recv)
-            for tick in range(1, ticks)
-            for half in range(2)
-            for k in range(row_n - 1)
-        ]
-
-    def target_copies():
-        return [
-            row_copy(2 * tick + half, k, aims.at[tick, half, mine], late_send, late_recv)
-            for tick in range(ticks - 1)
-            for half in range(2)
-            for k in range(row_n - 1)
-        ]
-
-    @pl.when(seg == 0)
-    def _():
-        for tick in range(1, ticks):
-            for half in range(2):
-                st[tick, SRC, half, mine] = fresh[tick, :, lanes(half)]
-        for copy in fresh_copies():
-            copy.start()
-
-    @pl.when(seg == seg_n - 1)
-    def _():
-        for tick in range(ticks - 1):
-            for half in range(2):
-                aims[tick, half, mine] = target[tick, :, lanes(half)]
-        for copy in target_copies():
-            copy.start()
+    for place in range(6):
+        at_place(place, lambda part: each(gathers(place, part), lambda copy: copy.start()))
+
+    def late_start(own, copies):
+        own().start()
+        each(copies, lambda copy: copy.start())
+
+    def late_landed(own, copies):
+        own().wait()
+        each(copies, lambda copy: copy.wait_recv())
+
+    def late_sent(own, copies):
+        each(copies, lambda copy: copy.wait_send())
+
+    def landed_at(places):
+        for place in places:
+
+            def wait(part):
+                own_copy(place, part).wait()
+                each(gathers(place, part), lambda copy: copy.wait_recv())
+
+            at_place(place, wait)
+
+    late_each(late_start)
 
     def store_kernel(ref, pair, tap, value):
         high, low = split_float(value)
@@ -158,11 +204,12 @@
     def prepare(index, carry):
         pair = index // 9
         tap = index - 9 * pair
-        value = weights[pair, pl.ds(pl.multiple_of(tap * chans, chans), chans), :]
+        value = held_weights[pair, pl.ds(pl.multiple_of(tap * chans, chans), chans), :]
         store_kernel(w_fwd, pair, tap, value)
         store_kernel(w_flip, pair, 8 - tap, value.T)
         return carry
 
+    weight_copy.wait()
     lax.fori_loop(0, 36, prepare, 0)
 
     rim = jnp.zeros((width, 2 * chans), jnp.bfloat16)
@@ -170,7 +217,7 @@
         for start in (0, width + cells):
             pad_fwd[side, start : start + width] = rim
             pad_src[side, start : start + width] = rim
-            for slot in range(4):
+            for slot in range(8):
                 pad_cot[slot, side, start : start + width] = rim
 
     column = lax.rem(lax.broadcasted_iota(jnp.int32, (cells, chans), 0), width)
@@ -199,58 +246,48 @@
     def pair_of(step):
         return 2 * (1 - step // 2) + 1 - step % 2
 
+    def slot_of(tick, step):
+        return 4 * (tick % 2) + step
+
     def forward_step(tick, step):
         even = step % 2 == 0
         source, goal = (1, 0) if even else (0, 1)
-        held = st if step < 2 else keep
-        if step == 0:
-            value = st[tick, SRC, source]
-        elif step == 1:
-            value = keep[source]
-        else:
-            value = keep[source]
+        value = st[tick, SRC, source] if step == 0 else keep[source]
         fill(pad_fwd, jax.nn.silu(value))
         base = st[tick, SRC, goal] if step < 2 else keep[goal]
-        fresh_value = base + conv(pad_fwd, w_fwd[step])
-        if step < 2:
-            keep[goal] = fresh_value
-        else:
-            chosen = jnp.where(doubled, fresh_value, keep[goal])
-            keep[goal] = fresh_value
-            produced[tick, SRC, goal] = chosen
+        value = base + conv(pad_fwd, w_fwd[step])
+        if step >= 2:
+            produced[tick, SRC, goal] = jnp.where(doubled, value, keep[goal])
+        keep[goal] = value
 
     def backward_open(tick, step):
         even = step % 2 == 0
-        held = (lambda f, h: st[tick, f, h]) if step == 0 else (lambda f, h: produced[tick, f, h])
-        if step == 0:
-            source, cot = st[tick, OUT, 0], st[tick, GRAD, 1]
-        elif even:
-            source, cot = produced[tick, OUT, 0], produced[tick, GRAD, 1]
-        else:
-            source, cot = produced[tick, OUT, 1], produced[tick, GRAD, 0]
-        if step == 1:
-            source, cot = produced[tick, OUT, 1], produced[tick, GRAD, 0]
+        holder = st if step == 0 else produced
+        source = holder[tick, OUT, 0 if even else 1]
+        cot = holder[tick, GRAD, 1 if even else 0]
         logistic = jax.nn.sigmoid(source)
         active = source * logistic
         fill(pad_src, active)
-        fill(pad_cot.at[step], cot)
+        fill(pad_cot.at[slot_of(tick, step)], cot)
         high, low = split_float(active.T)
-        src_t[step, :chans] = high
-        src_t[step, chans:] = low
+        src_t[slot_of(tick, step), :chans] = high
+        src_t[slot_of(tick, step), chans:] = low
         return logistic * (1.0 + source * (1.0 - logistic))
 
-    def backward_close(tick, step, slope):
+    def backward_close(tick, step, slope, send):
         even = step % 2 == 0
         out_goal, grad_goal = (1, 0) if even else (0, 1)
         holder = st if step < 2 else produced
         out_old = holder[tick, OUT, out_goal]
         grad_old = holder[tick, GRAD, grad_goal]
         rebuilt = conv(pad_src, w_fwd[pair_of(step)])
-        added = conv(pad_cot.at[step], w_flip[pair_of(step)]) * slope
-        out_new = out_old - rebuilt
-        grad_new = grad_old + added
-        produced[tick, OUT, out_goal] = out_new
-        produced[tick, GRAD, grad_goal] = grad_new
+        produced[tick, OUT, out_goal] = out_old - rebuilt
+        if send and step >= 2:
+            seg_start(tick, OUT, out_goal)
+        added = conv(pad_cot.at[slot_of(tick, step)], w_flip[pair_of(step)]) * slope
+        produced[tick, GRAD, grad_goal] = grad_old + added
+        if send and step >= 2:
+            seg_start(tick, GRAD, grad_goal)
         if step == 1:
             for half in range(2):
                 for field in (OUT, GRAD):
@@ -266,8 +303,8 @@
             other = 8 - first_tap - extra
             down = other // 3
             side = other - 3 * down
-            cots = pad_cot[step, side, pl.ds(pl.multiple_of(down * width, width), cells), :]
-            four = jnp.dot(src_t[step], cots, preferred_element_type=jnp.float32)
+            cots = pad_cot[slot_of(tick, step), side, pl.ds(pl.multiple_of(down * width, width), cells), :]
+            four = jnp.dot(src_t[slot_of(tick, step)], cots, preferred_element_type=jnp.float32)
             two = four[:chans] + four[chans:]
             value = two[:, :chans] + two[:, chans:]
             rows = slice(extra * chans, (extra + 1) * chans)
@@ -354,49 +391,37 @@
     for tick in range(ticks):
         final = tick == ticks - 1
         for step in range(4):
-            if tick == 0:
-                if step == 0:
-                    for place in range(3):
-                        for copy in gathers(place):
-                            copy.wait_recv()
-            elif step == 0:
-                seg_wait_recv(tick - 1, OUT, 0)
-                seg_wait_recv(tick - 1, GRAD, 1)
+            if step == 0:
+                if tick == 0:
+                    landed_at((0, 1))
+                else:
+                    seg_wait_recv(tick - 1, OUT, 0)
+                    seg_wait_recv(tick - 1, GRAD, 1)
             slope = backward_open(tick, step)
             if final:
                 kernel_grads(tick, step)
                 red_start(pair_of(step), 0)
             if step == 0:
                 if tick == 0:
-                    for place in range(3, 6):
-                        for copy in gathers(place):
-                            copy.wait_recv()
+                    landed_at((2, 3))
                 else:
                     seg_wait_recv(tick - 1, OUT, 1)
                     seg_wait_recv(tick - 1, GRAD, 0)
-            if not final:
-                if step == 0 and tick > 0:
-                    seg_wait_recv(tick - 1, SRC, 0)
-                    seg_wait_recv(tick - 1, SRC, 1)
-                forward_step(tick, step)
-            backward_close(tick, step, slope)
+            backward_close(tick, step, slope, not final)
+        if tick == 0:
+            landed_at((4, 5))
+            late_each(late_landed)
+        else:
+            seg_wait_recv(tick - 1, SRC, 0)
+            seg_wait_recv(tick - 1, SRC, 1)
+        for step in range(4):
+            if final and levels > 0:
+                red_finish(pair_of(step), 0)
+                red_start(pair_of(step), 1)
+            forward_step(tick, step)
             if not final and step >= 2:
-                even = step % 2 == 0
-                seg_start(tick, SRC, 0 if even else 1)
-                seg_start(tick, OUT, 1 if even else 0)
-                seg_start(tick, GRAD, 0 if even else 1)
+                seg_start(tick, SRC, step % 2)
         if not final:
-            if tick == 0:
-
-                @pl.when(seg == 0)
-                def _():
-                    for copy in fresh_copies():
-                        copy.wait_recv()
-
-                @pl.when(seg == seg_n - 1)
-                def _():
-                    for copy in target_copies():
-                        copy.wait_recv()
 
             @pl.when(seg == seg_n - 1)
             def _(tick=tick):
@@ -407,15 +432,6 @@
 
             for step in range(4):
                 kernel_grads(tick, step)
-        else:
-            if tick > 0:
-                seg_wait_recv(tick - 1, SRC, 0)
-                seg_wait_recv(tick - 1, SRC, 1)
-            for step in range(4):
-                if levels > 0:
-                    red_finish(pair_of(step), 0)
-                    red_start(pair_of(step), 1)
-                forward_step(tick, step)
 
     last = ticks - 1
     for half in range(2):
@@ -435,19 +451,8 @@
         grads_out[pair] = total
 
     for place in range(6):
-        for copy in gathers(place):
-            copy.wait_send()
-
-    @pl.when(seg == 0)
-    def _():
-        for copy in fresh_copies():
-            copy.wait_send()
-
-    @pl.when(seg == seg_n - 1)
-    def _():
-        for copy in target_copies():
-            copy.wait_send()
-
+        at_place(place, lambda part: each(gathers(place, part), lambda copy: copy.wait_send()))
+    late_each(late_sent)
     for tick in range(ticks - 1):
         for field in (SRC, OUT, GRAD):
             for half in range(2):
@@ -486,7 +491,7 @@
             jax.ShapeDtypeStruct((local, both), f32),
             jax.ShapeDtypeStruct((2, local, both), f32),
         ),
-        in_specs=[vmem] * 5 + [pl.BlockSpec(memory_space=pltpu.SMEM)],
+        in_specs=[pl.BlockSpec(memory_space=pltpu.HBM)] * 5 + [pl.BlockSpec(memory_space=pltpu.SMEM)],
         out_specs=(vmem, vmem, vmem),
         scratch_shapes=[
             pltpu.VMEM((ticks, 3, 2, cells, chans), f32),
@@ -497,8 +502,8 @@
             pltpu.VMEM((pairs, 18 * chans, 2 * chans), b16),
             pltpu.VMEM((3, padded, 2 * chans), b16),
             pltpu.VMEM((3, padded, 2 * chans), b16),
-            pltpu.VMEM((4, 3, padded, 2 * chans), b16),
-            pltpu.VMEM((4, 2 * chans, cells), b16),
+            pltpu.VMEM((8, 3, padded, 2 * chans), b16),
+            pltpu.VMEM((8, 2 * chans, cells), b16),
             pltpu.VMEM((pairs, taps * chans, chans), f32),
             pltpu.VMEM((pairs, max(reach, 1), chunk, chans), f32),
             dma((6, peers)),
@@ -509,10 +514,14 @@
             dma((6 * ticks,)),
             dma((pairs, max(reach, 1))),
             dma((pairs, max(reach, 1))),
+            pltpu.VMEM((pairs, 9 * chans, chans), f32),
+            dma((6,)),
+            dma((late,)),
+            dma((1,)),
         ],
         cost_estimate=pl.CostEstimate(flops=flops, bytes_accessed=1 << 22, transcendentals=1 << 20),
         compiler_params=pltpu.CompilerParams(
-            collective_id=0, has_side_effects=True, vmem_limit_bytes=48 << 20
+            collective_id=0, has_side_effects=True, vmem_limit_bytes=62 << 20
         ),
     )(
         fresh.reshape(ticks, local, both),

time: 54.5 us -> 53.3 us (0.978)
  local copies, waits for them, and re-layouts: 7.44 us -> 4.93 us
  Pallas kernels: 45.5 us -> 46.9 us
    unnamed x13 -> x3, local copies, waits for them, and re-layouts: 7.44 us -> 4.93 us
    pallas_call x1, Pallas kernels: 45.5 us -> 46.9 us  [per_device(): pl.pallas_call(functools.partial(kernel_body, sizes), out_shape=(jax.Shap...]
where the time goes in v2:
time: 53.3 us; the launch traced here: 53.1 us
  Pallas kernels  46.9 us (88%)
  local copies, waits for them, and re-layouts  4.93 us (9%)
  between operations  1.29 us (2%)
    pallas_call x1, Pallas kernels, per_device(): pl.pallas_call(functools.partial(kernel_body, sizes), out_shape=(jax.Shap...  46.9 us
    unnamed x3, local copies, waits for them, and re-layouts  4.93 us

profile of v2, /device:TPU:1, one launch (start us, length us, event | category | flops | bytes accessed | tf_op | source)
XLA Modules:
  0.0 53.1 jit_solution(16662090838092760242)
XLA Ops:
  1.3 46.9 %shard_map.85 = (f32[4,144,128]{2,1,0:T(8,128)}, f32[128,256]{1,0:T(8,128)}, f32[2,128,256]{2,1,0:T(8,128)}) custom-call(f32[2,128,256]{2,1,0:T(8,128)} %bitcast.14, f32[1,128,256]{2,1,0:T(8,128)} %bitcast.16, f32[128,256]{1,0:T(8,128)} %bitcast.17, f32[2,128,256]{2,1,0:T(8,128)} %bitcast.15, f32[4,1152,128]{2,1,0:T(8,128)} %bitcast.13, s32[1]{0:T(128)S(6)} %copy.13.blocks), custom_call_target="tpu_custom_call" | custom-call | flops 8589934592 | bytes 4194304 | tf_op jit(solution)/shard_map/pallas_call | solution.py:487
  48.1 1.7 %copy.14 = f32[1,2,2,144,128]{4,3,2,1,0:T(8,128)} copy(f32[1,2,2,144,128]{4,3,2,1,0:T(8,128)} %bitcast.10) | data formatting | bytes 589824
  49.8 1.6 %copy.15 = f32[1,1,8,16,256]{4,3,2,1,0:T(8,128)} copy(f32[1,1,8,16,256]{4,3,2,1,0:T(8,128)} %bitcast.12) | data formatting | bytes 262144
  51.4 1.7 %copy.16 = f32[1,2,1,8,16,256]{5,4,3,2,1,0:T(8,128)} copy(f32[1,2,1,8,16,256]{5,4,3,2,1,0:T(8,128)} %bitcast.11) | data formatting | bytes 524288
